TPU v7x, 128 devices: a whole 4x4x4 slice. The times are simulated.
128 devices in a mesh: dp: 32 (over x, z, core), mp: 4 (over y).
Axes of the slice: x: 4, y: 4, z: 4, core: 2. Of those that a mesh axis runs over, the one named last changes fastest.
Arguments:
- embedding: bfloat16 [8192, 7168], P('dp', 'mp'), may hold values from -6 to 6
- hidden: bfloat16 [8192, 7168], P('dp', 'mp'), may hold values from -6 to 6
- embed_gain: float32 [7168], P('mp'), may hold values from 0.3 to 1.7
- hidden_gain: float32 [7168], P('mp'), may hold values from 0.3 to 1.7
- cotangent: bfloat16 [8192, 4096], P('dp', 'mp'), may hold values from -0.015625 to 0.015625
- left_stat: float32 [32768, 4096], P('dp', 'mp'), may hold values from -6 to 6
- right_stat: float32 [32768, 4096], P('dp', 'mp'), may hold values from -6 to 6
- left_root: bfloat16 [32768, 4096], P('dp', 'mp')
- right_root: bfloat16 [32768, 4096], P('dp', 'mp')
- owners: int32 [4, 14], replicated, may hold values from 0 to 31, as said below
Outputs:
- left_new: float32 [32768, 4096], P('dp', 'mp')
- right_new: float32 [32768, 4096], P('dp', 'mp')
- update: bfloat16 [4, 1024, 14336], P('mp', 'dp')
Inputs may be any that keep to these rules, and one draw needn't show every extreme that they name: In each block column the 14 owners are all different.
All inputs are finite; a program needn't handle non-finite values.
Results may differ from a plain program's by a relative error of at most 0.023.
Values may be sent and summed in bfloat16 or wider, within the bound.
A program may use at most 192 MiB of HBM per device.

v0:
```python
import jax
import jax.numpy as jnp
from jax import lax
from jax.sharding import PartitionSpec as P


def body(
    embedding,
    hidden,
    embed_gain,
    hidden_gain,
    cotangent,
    left_stat,
    right_stat,
    left_root,
    right_root,
    owners,
):
    stacked = jnp.stack([embedding, hidden], axis=1)
    values = stacked.astype(jnp.float32)
    squares = lax.psum(jnp.sum(values * values, axis=2), "mp")
    width = hidden.shape[1] * lax.axis_size("mp")
    scale = lax.rsqrt(squares / width + 1e-06)
    gains = jnp.stack([embed_gain, hidden_gain], axis=0)
    normed = (values * scale[:, :, None] * gains[None, :, :]).astype(jnp.bfloat16)
    total_in = 2 * width
    replicas = lax.axis_size("dp")
    side = cotangent.shape[1]
    sliver = side // replicas
    partial_value = jnp.einsum(
        "tb,thk->bhk",
        cotangent,
        lax.all_gather(normed, "mp", axis=2, tiled=True),
        preferred_element_type=jnp.float32,
    )
    share = lax.psum_scatter(
        partial_value.reshape(side, total_in).astype(jnp.bfloat16),
        "dp",
        scatter_dimension=0,
        tiled=True,
    ).astype(jnp.float32)
    share = share.astype(jnp.bfloat16)
    block_rows = total_in // side
    my_replica = lax.axis_index("dp")
    my_column = lax.axis_index("mp")
    column_owners = lax.dynamic_index_in_dim(owners, my_column, 0, keepdims=False)
    owner_hot = (column_owners[None, :] == jnp.arange(replicas, dtype=jnp.int32)[:, None]).astype(
        jnp.bfloat16
    )
    pieces = share.reshape(sliver, block_rows, side)
    outgoing = jnp.einsum(
        "or,srb->osb", owner_hot, pieces, preferred_element_type=jnp.float32
    ).astype(jnp.bfloat16)
    arrived = lax.all_to_all(outgoing, "dp", split_axis=0, concat_axis=1, tiled=True)
    grad_t = arrived.reshape(side, side)
    owned = jnp.any(column_owners == my_replica)
    gram_left = lax.dot_general(
        grad_t, grad_t, (((0,), (0,)), ((), ())), preferred_element_type=jnp.float32
    )
    gram_right = lax.dot_general(
        grad_t, grad_t, (((1,), (1,)), ((), ())), preferred_element_type=jnp.float32
    )
    left_new = jnp.where(owned, 0.9 * left_stat + 0.1 * gram_left, left_stat)
    right_new = jnp.where(owned, 0.9 * right_stat + 0.1 * gram_right, right_stat)
    inner_t = lax.dot_general(
        right_root, grad_t, (((0,), (0,)), ((), ())), preferred_element_type=jnp.float32
    ).astype(jnp.bfloat16)
    result_t = lax.dot_general(
        inner_t, left_root, (((1,), (1,)), ((), ())), preferred_element_type=jnp.float32
    ).astype(jnp.bfloat16)
    returned = lax.all_to_all(
        result_t.reshape(replicas, sliver, side), "dp", split_axis=0, concat_axis=0, tiled=True
    )
    placed = jnp.einsum(
        "or,osb->srb", owner_hot, returned, preferred_element_type=jnp.float32
    ).astype(jnp.bfloat16)
    update = placed.reshape(1, sliver, total_in)
    return (left_new, right_new, update)


def solution(mesh):
    placed = (
        P("dp", "mp"),
        P("dp", "mp"),
        P("mp"),
        P("mp"),
        P("dp", "mp"),
        P("dp", "mp"),
        P("dp", "mp"),
        P("dp", "mp"),
        P("dp", "mp"),
        P(),
    )
    return jax.shard_map(
        body,
        mesh=mesh,
        in_specs=placed,
        out_specs=(P("dp", "mp"), P("dp", "mp"), P("mp", "dp", None)),
        check_vma=False,
    )
```

profile of v0, /device:TPU:1, one launch (start us, length us, event | category | flops | bytes accessed | tf_op | source)
XLA Modules:
  0.0 399.5 jit_solution(72349972238462122)
XLA Ops:
  7.2 0.0 copy-start
  7.2 0.0 all-gather.2.cloned.1.call-start
  7.2 0.8 stack.22
  8.1 0.7 stack.21
  8.8 1.5 copy.27
  10.2 2.2 copy.26
  12.4 1.6 fusion.2
  14.0 9.6 %psum.7 = f32[256,2]{0,1:T(2,128)S(1)} all-reduce(f32[256,2]{0,1:T(2,128)S(1)} %fusion.2), channel_id=1, replica_groups=mesh['dp'=32,'mp'=4] {'mp'}, use_global_device_ids=true, to_apply=%region_2.0 | all-reduce | flops 512 | bytes 4096 | tf_op jit(solution)/shard_map/psum | solution.py:21
  23.6 0.0 copy-start.4
  23.6 2.6 fusion.4
  26.3 0.0 all-gather.2.cloned.1.call-update
  26.3 0.0 reduce-scatter.2.cloned.1.call-start
  26.3 76.6 %all-gather.2.cloned.1.call-done = bf16[256,2,7168]{0,2,1:T(8,128)(2,1)} async-done(((bf16[256,2,1792]{0,2,1:T(8,128)(2,1)}), bf16[256,2,7168]{0,2,1:T(8,128)(2,1)}) %all-gather.2.cloned.1.call-update) | async-done | bytes 7340048 | tf_op jit(solution)/shard_map/all_gather | solution.py:33
  102.9 15.7 %convolution_convert_fusion = bf16[2,7168,1024]{2,1,0:T(8,128)(2,1)} fusion(bf16[256,2,7168]{0,2,1:T(8,128)(2,1)} %all-gather.2.cloned.1.call-done, bf16[256,1024]{1,0:T(8,128)(2,1)S(1)} %copy-done.4), kind=kOutput, calls=%fused_computation | convolution fusion | flops 7530872832 | bytes 37224448 | tf_op jit(solution)/shard_map/tb,thk->bhk/dot_general | solution.py:30
  118.6 36.3 %copy.28 = bf16[1024,14336]{1,0:T(8,128)(2,1)} copy(bf16[1024,14336]{0,1:T(8,128)(2,1)} %bitcast.34) | data formatting | bytes 58720256 | tf_op jit(solution)/shard_map/convert_element_type | solution.py:37
  154.9 0.0 reduce-scatter.2.cloned.1.call-update
  154.9 1.3 compare_reduce_fusion
  156.3 153.0 %reduce-scatter.2.cloned.1.call-done = bf16[32,14336]{1,0:T(8,128)(2,1)} async-done(((bf16[1024,14336]{1,0:T(8,128)(2,1)}), bf16[32,14336]{1,0:T(8,128)(2,1)}) %reduce-scatter.2.cloned.1.call-update) | async-done | bytes 917520 | tf_op jit(solution)/shard_map/reduce_scatter | solution.py:36
  309.3 1.9 reshape.26
  311.2 0.8 convolution_convert_fusion.1
  312.0 1.2 copy.29
  313.2 33.5 %all_to_all.14 = bf16[32,32,1024]{2,1,0:T(8,128)(2,1)} all-to-all(bf16[32,32,1024]{2,1,0:T(8,128)(2,1)S(1)} %copy.29), channel_id=1, replica_groups=mesh['dp'=32,'mp'=4] {'dp'}, dimensions={0} | all-to-all | bytes 4194304 | tf_op jit(solution)/shard_map/all_to_all | solution.py:54
  346.7 8.1 %fusion.9 = bf16[1024,1024]{1,0:T(8,128)(2,1)} fusion(bf16[1024,1024]{1,0:T(8,128)(2,1)S(1)} %copy-done, bf16[1024,1024]{1,0:T(8,128)(2,1)} %bitcast.39, bf16[1024,1024]{1,0:T(8,128)(2,1)} %param.18), kind=kOutput, calls=%fused_computation.14 | convolution fusion | flops 4297064448 | bytes 8388608 | tf_op jit(solution)/shard_map/dot_general | solution.py:68
  354.8 4.9 %all-to-all-start.1 = ((bf16[32,32,1024]{2,1,0:T(8,128)(2,1)}), bf16[32,32,1024]{2,1,0:T(8,128)(2,1)}, u32[]{:S(2)}, u32[]{:S(2)}) async-start(bf16[32,32,1024]{2,1,0:T(8,128)(2,1)} %bitcast.41), calls=%async_computation.2 | async-start | bytes 4194304 | tf_op jit(solution)/shard_map/all_to_all | solution.py:71
  359.7 0.0 copy-done.2
  359.7 0.0 copy-start.3
  359.7 0.0 copy-start.5
  359.7 8.0 %add_select_fusion = f32[1024,1024]{1,0:T(8,128)} fusion(f32[1024,1024]{1,0:T(8,128)} %param.16, bf16[1024,1024]{1,0:T(8,128)(2,1)S(1)} %bitcast.40, pred[]{:T(512)} %get-tuple-element.3), kind=kOutput, calls=%fused_computation.6 | convolution fusion | flops 2151677952 | bytes 10485761 | tf_op jit(solution)/shard_map/dot_general | solution.py:60
  367.7 5.5 %fusion.1 = f32[1024,1024]{1,0:T(8,128)} fusion(f32[1024,1024]{1,0:T(8,128)S(1)} %copy-done.5, bf16[32,32,1024]{2,1,0:T(8,128)(2,1)S(1)} %copy-done.3, pred[]{:T(512)} %get-tuple-element.3), kind=kOutput, calls=%fused_computation.5 | convolution fusion | flops 2151677952 | bytes 10485761 | tf_op jit(solution)/shard_map/dot_general | solution.py:57
  373.2 14.8 %all-to-all-done.1 = bf16[32,32,1024]{2,1,0:T(8,128)(2,1)} async-done(((bf16[32,32,1024]{2,1,0:T(8,128)(2,1)}), bf16[32,32,1024]{2,1,0:T(8,128)(2,1)}, u32[]{:S(2)}, u32[]{:S(2)}) %all-to-all-start.1) | async-done | bytes 2097184 | tf_op jit(solution)/shard_map/all_to_all | solution.py:71
  388.0 2.9 fusion.15
  390.9 1.7 reshape.29
  (9 shorter events, 0.0 us)
Async XLA Ops:
  7.2 339.6 %copy-start = (bf16[1024,1024]{1,0:T(8,128)(2,1)S(1)}, bf16[1024,1024]{1,0:T(8,128)(2,1)}, u32[]{:S(2)}) copy-start(bf16[1024,1024]{1,0:T(8,128)(2,1)} %param.17) | copy-start | bytes 6291460
  7.2 95.7 %all-gather.2.cloned.1.call-start = ((), (), s32[]{:S(2)}) async-start(), calls=%async_computation.3 | async-start | bytes 9175040 | tf_op jit(solution)/shard_map/all_gather | solution.py:33
  23.6 79.3 %copy-start.4 = (bf16[256,1024]{1,0:T(8,128)(2,1)S(1)}, bf16[256,1024]{1,0:T(8,128)(2,1)}, u32[]{:S(2)}) copy-start(bf16[256,1024]{1,0:T(8,128)(2,1)} %param.14) | copy-start | bytes 1572868
  26.3 283.0 %reduce-scatter.2.cloned.1.call-start = ((), (), s32[]{:S(2)}) async-start(), calls=%async_computation.4 | async-start | bytes 30277632 | tf_op jit(solution)/shard_map/reduce_scatter | solution.py:36
  354.8 4.9 %copy-start.2 = (bf16[32,32,1024]{2,1,0:T(8,128)(2,1)S(1)}, bf16[32,32,1024]{2,1,0:T(8,128)(2,1)}, u32[]{:S(2)}) copy-start(bf16[32,32,1024]{2,1,0:T(8,128)(2,1)} %all_to_all.14) | copy-start | bytes 6291460
  354.8 33.2 %all-to-all-start.1 = ((bf16[32,32,1024]{2,1,0:T(8,128)(2,1)}), bf16[32,32,1024]{2,1,0:T(8,128)(2,1)}, u32[]{:S(2)}, u32[]{:S(2)}) async-start(bf16[32,32,1024]{2,1,0:T(8,128)(2,1)} %bitcast.41), calls=%async_computation.2 | async-start | bytes 4194304 | tf_op jit(solution)/shard_map/all_to_all | solution.py:71
  359.7 8.0 %copy-start.3 = (bf16[32,32,1024]{2,1,0:T(8,128)(2,1)S(1)}, bf16[32,32,1024]{2,1,0:T(8,128)(2,1)}, u32[]{:S(2)}) copy-start(bf16[32,32,1024]{2,1,0:T(8,128)(2,1)} %all_to_all.14) | copy-start | bytes 6291460
  359.7 8.0 %copy-start.5 = (f32[1024,1024]{1,0:T(8,128)S(1)}, f32[1024,1024]{1,0:T(8,128)}, u32[]{:S(2)}) copy-start(f32[1024,1024]{1,0:T(8,128)} %param.15) | copy-start | bytes 12582916
  367.7 24.9 %copy-start.1 = (bf16[1024,1024]{1,0:T(8,128)(2,1)S(1)}, bf16[1024,1024]{1,0:T(8,128)(2,1)}, u32[]{:S(2)}) copy-start(bf16[1024,1024]{1,0:T(8,128)(2,1)} %param.17) | copy-start | bytes 6291460
Sparse Core Ops, SparseCore 0:
  26.4 76.4 all-gather.1
  155.1 154.2 reduce-scatter.1
where the time goes:
time: 401 us; the launch traced here: 399 us
  waiting for transfers between devices  244 us (61%)
  local copies, waits for them, and re-layouts  46.4 us (12%)
  blocking collectives  43.1 us (11%)
  matrix products  40.9 us (10%)
  between operations  14.1 us (4%)
  other arithmetic  5.57 us (1%)
  starting transfers between devices  4.94 us (1%)
    reduce_scatter x1, waiting for transfers between devices, body(): lax.psum_scatter(partial_value.reshape(side, total_in).astype(jnp.bfloat1...  153 us
    all_gather x1, waiting for transfers between devices, body(): lax.all_gather(normed, 'mp', axis=2, tiled=True)  76.6 us
    convert_element_type x1, local copies, waits for them, and re-layouts, body(): partial_value.reshape(side, total_in).astype(jnp.bfloat16)  36.3 us
    all_to_all x1, blocking collectives, body(): lax.all_to_all(outgoing, 'dp', split_axis=0, concat_axis=1, tiled=True)  33.5 us
    dot_general x1, matrix products, body(): jnp.einsum('tb,thk->bhk', cotangent, lax.all_gather(normed, 'mp', axis=2,...  15.7 us
    all_to_all x1, waiting for transfers between devices, body(): lax.all_to_all(result_t.reshape(replicas, sliver, side), 'dp', split_axis...  14.8 us
    psum x1, blocking collectives, body(): squares = lax.psum(jnp.sum(values * values, axis=2), 'mp')  9.55 us
    dot_general x1, matrix products, body(): lax.dot_general(inner_t, left_root, (((1,), (1,)), ((), ())), preferred_e...  8.09 us
  transfers between devices with their start and end apart: 3, of which 3 were waited for; matrix products, arithmetic and copies ran while one was open for 4% of the time, Pallas kernels for 0%

commit v1 on v0

--- a/solution.py
+++ b/solution.py
@@ -18,7 +18,7 @@
 ):
     stacked = jnp.stack([embedding, hidden], axis=1)
     values = stacked.astype(jnp.float32)
-    squares = lax.psum(jnp.sum(values * values, axis=2), "mp")
+    squares = jnp.sum(lax.all_gather(jnp.sum(values * values, axis=2), "mp"), axis=0)
     width = hidden.shape[1] * lax.axis_size("mp")
     scale = lax.rsqrt(squares / width + 1e-06)
     gains = jnp.stack([embed_gain, hidden_gain], axis=0)

time: 401 us -> 403 us (level)
    psum x1 -> x0, blocking collectives: 9.55 us -> none  [body(): squares = lax.psum(jnp.sum(values * values, axis=2), 'mp')]
    all_gather x0 -> x1, blocking collectives: none -> 9.42 us  [body(): lax.all_gather(jnp.sum(values * values, axis=2), 'mp')]
where the time goes in v1:
time: 403 us; the launch traced here: 401 us
  waiting for transfers between devices  246 us (61%)
  local copies, waits for them, and re-layouts  46.4 us (12%)
  blocking collectives  42.9 us (11%)
  matrix products  40.9 us (10%)
  between operations  14.1 us (3%)
  other arithmetic  5.6 us (1%)
  starting transfers between devices  4.94 us (1%)
    reduce_scatter x1, waiting for transfers between devices, body(): lax.psum_scatter(partial_value.reshape(side, total_in).astype(jnp.bfloat1...  153 us
    all_gather x1, waiting for transfers between devices, body(): lax.all_gather(normed, 'mp', axis=2, tiled=True)  78.4 us
    convert_element_type x1, local copies, waits for them, and re-layouts, body(): partial_value.reshape(side, total_in).astype(jnp.bfloat16)  36.3 us
    all_to_all x1, blocking collectives, body(): lax.all_to_all(outgoing, 'dp', split_axis=0, concat_axis=1, tiled=True)  33.5 us
    dot_general x1, matrix products, body(): jnp.einsum('tb,thk->bhk', cotangent, lax.all_gather(normed, 'mp', axis=2,...  15.7 us
    all_to_all x1, waiting for transfers between devices, body(): lax.all_to_all(result_t.reshape(replicas, sliver, side), 'dp', split_axis...  14.8 us
    all_gather x1, blocking collectives, body(): lax.all_gather(jnp.sum(values * values, axis=2), 'mp')  9.42 us
    dot_general x1, matrix products, body(): lax.dot_general(inner_t, left_root, (((1,), (1,)), ((), ())), preferred_e...  8.09 us
  transfers between devices with their start and end apart: 3, of which 3 were waited for; matrix products, arithmetic and copies ran while one was open for 4% of the time, Pallas kernels for 0%

profile of v1, /device:TPU:1, one launch (start us, length us, event | category | flops | bytes accessed | tf_op | source)
XLA Modules:
  0.0 401.2 jit_solution(11350637236911960299)
XLA Ops:
  7.2 0.0 copy-start
  7.2 0.0 all-gather.3.cloned.1.call-start
  7.2 0.8 stack.22
  8.1 0.7 stack.21
  8.8 1.5 copy.27
  10.2 2.2 copy.26
  12.4 1.6 fusion.2
  14.0 9.4 %all-gather = f32[1024,2]{0,1:T(2,128)S(1)} all-gather(f32[256,2]{0,1:T(2,128)S(1)} %fusion.2), channel_id=2, replica_groups=mesh['dp'=32,'mp'=4] {'mp'}, dimensions={0}, use_global_device_ids=true | all-gather | bytes 10240 | tf_op jit(solution)/shard_map/all_gather | solution.py:21
  23.5 0.0 copy-start.4
  23.5 2.6 fusion.4
  26.2 0.0 all-gather.3.cloned.1.call-update
  26.2 0.0 reduce-scatter.2.cloned.1.call-start
  26.3 78.4 %all-gather.3.cloned.1.call-done = bf16[256,2,7168]{0,2,1:T(8,128)(2,1)} async-done(((bf16[256,2,1792]{0,2,1:T(8,128)(2,1)}), bf16[256,2,7168]{0,2,1:T(8,128)(2,1)}) %all-gather.3.cloned.1.call-update) | async-done | bytes 7340048 | tf_op jit(solution)/shard_map/all_gather | solution.py:33
  104.7 15.7 %convolution_convert_fusion = bf16[2,7168,1024]{2,1,0:T(8,128)(2,1)} fusion(bf16[256,2,7168]{0,2,1:T(8,128)(2,1)} %all-gather.3.cloned.1.call-done, bf16[256,1024]{1,0:T(8,128)(2,1)S(1)} %copy-done.4), kind=kOutput, calls=%fused_computation | convolution fusion | flops 7530872832 | bytes 37224448 | tf_op jit(solution)/shard_map/tb,thk->bhk/dot_general | solution.py:30
  120.3 36.3 %copy.28 = bf16[1024,14336]{1,0:T(8,128)(2,1)} copy(bf16[1024,14336]{0,1:T(8,128)(2,1)} %bitcast.36) | data formatting | bytes 58720256 | tf_op jit(solution)/shard_map/convert_element_type | solution.py:37
  156.7 0.0 reduce-scatter.2.cloned.1.call-update
  156.7 1.3 compare_reduce_fusion
  158.0 153.0 %reduce-scatter.2.cloned.1.call-done = bf16[32,14336]{1,0:T(8,128)(2,1)} async-done(((bf16[1024,14336]{1,0:T(8,128)(2,1)}), bf16[32,14336]{1,0:T(8,128)(2,1)}) %reduce-scatter.2.cloned.1.call-update) | async-done | bytes 917520 | tf_op jit(solution)/shard_map/reduce_scatter | solution.py:36
  311.1 1.9 reshape.30
  313.0 0.8 convolution_convert_fusion.1
  313.8 1.2 copy.29
  314.9 33.5 %all_to_all.14 = bf16[32,32,1024]{2,1,0:T(8,128)(2,1)} all-to-all(bf16[32,32,1024]{2,1,0:T(8,128)(2,1)S(1)} %copy.29), channel_id=1, replica_groups=mesh['dp'=32,'mp'=4] {'dp'}, dimensions={0} | all-to-all | bytes 4194304 | tf_op jit(solution)/shard_map/all_to_all | solution.py:54
  348.5 8.1 %fusion.9 = bf16[1024,1024]{1,0:T(8,128)(2,1)} fusion(bf16[1024,1024]{1,0:T(8,128)(2,1)S(1)} %copy-done, bf16[1024,1024]{1,0:T(8,128)(2,1)} %bitcast.41, bf16[1024,1024]{1,0:T(8,128)(2,1)} %param.18), kind=kOutput, calls=%fused_computation.14 | convolution fusion | flops 4297064448 | bytes 8388608 | tf_op jit(solution)/shard_map/dot_general | solution.py:68
  356.6 4.9 %all-to-all-start.1 = ((bf16[32,32,1024]{2,1,0:T(8,128)(2,1)}), bf16[32,32,1024]{2,1,0:T(8,128)(2,1)}, u32[]{:S(2)}, u32[]{:S(2)}) async-start(bf16[32,32,1024]{2,1,0:T(8,128)(2,1)} %bitcast.43), calls=%async_computation.2 | async-start | bytes 4194304 | tf_op jit(solution)/shard_map/all_to_all | solution.py:71
  361.4 0.0 copy-done.2
  361.4 0.0 copy-start.3
  361.4 0.0 copy-start.5
  361.5 8.0 %add_select_fusion = f32[1024,1024]{1,0:T(8,128)} fusion(f32[1024,1024]{1,0:T(8,128)} %param.16, bf16[1024,1024]{1,0:T(8,128)(2,1)S(1)} %bitcast.42, pred[]{:T(512)} %get-tuple-element.3), kind=kOutput, calls=%fused_computation.6 | convolution fusion | flops 2151677952 | bytes 10485761 | tf_op jit(solution)/shard_map/dot_general | solution.py:60
  369.4 5.5 %fusion.1 = f32[1024,1024]{1,0:T(8,128)} fusion(f32[1024,1024]{1,0:T(8,128)S(1)} %copy-done.5, bf16[32,32,1024]{2,1,0:T(8,128)(2,1)S(1)} %copy-done.3, pred[]{:T(512)} %get-tuple-element.3), kind=kOutput, calls=%fused_computation.5 | convolution fusion | flops 2151677952 | bytes 10485761 | tf_op jit(solution)/shard_map/dot_general | solution.py:57
  374.9 14.8 %all-to-all-done.1 = bf16[32,32,1024]{2,1,0:T(8,128)(2,1)} async-done(((bf16[32,32,1024]{2,1,0:T(8,128)(2,1)}), bf16[32,32,1024]{2,1,0:T(8,128)(2,1)}, u32[]{:S(2)}, u32[]{:S(2)}) %all-to-all-start.1) | async-done | bytes 2097184 | tf_op jit(solution)/shard_map/all_to_all | solution.py:71
  389.8 2.9 fusion.15
  392.7 1.7 reshape.33
  (11 shorter events, 0.1 us)
Async XLA Ops:
  7.2 341.3 %copy-start = (bf16[1024,1024]{1,0:T(8,128)(2,1)S(1)}, bf16[1024,1024]{1,0:T(8,128)(2,1)}, u32[]{:S(2)}) copy-start(bf16[1024,1024]{1,0:T(8,128)(2,1)} %param.17) | copy-start | bytes 6291460
  7.2 97.5 %all-gather.3.cloned.1.call-start = ((), (), s32[]{:S(2)}) async-start(), calls=%async_computation.3 | async-start | bytes 9175040 | tf_op jit(solution)/shard_map/all_gather | solution.py:33
  23.5 81.1 %copy-start.4 = (bf16[256,1024]{1,0:T(8,128)(2,1)S(1)}, bf16[256,1024]{1,0:T(8,128)(2,1)}, u32[]{:S(2)}) copy-start(bf16[256,1024]{1,0:T(8,128)(2,1)} %param.14) | copy-start | bytes 1572868
  26.2 284.9 %reduce-scatter.2.cloned.1.call-start = ((), (), s32[]{:S(2)}) async-start(), calls=%async_computation.4 | async-start | bytes 30277632 | tf_op jit(solution)/shard_map/reduce_scatter | solution.py:36
  356.6 4.9 %copy-start.2 = (bf16[32,32,1024]{2,1,0:T(8,128)(2,1)S(1)}, bf16[32,32,1024]{2,1,0:T(8,128)(2,1)}, u32[]{:S(2)}) copy-start(bf16[32,32,1024]{2,1,0:T(8,128)(2,1)} %all_to_all.14) | copy-start | bytes 6291460
  356.6 33.2 %all-to-all-start.1 = ((bf16[32,32,1024]{2,1,0:T(8,128)(2,1)}), bf16[32,32,1024]{2,1,0:T(8,128)(2,1)}, u32[]{:S(2)}, u32[]{:S(2)}) async-start(bf16[32,32,1024]{2,1,0:T(8,128)(2,1)} %bitcast.43), calls=%async_computation.2 | async-start | bytes 4194304 | tf_op jit(solution)/shard_map/all_to_all | solution.py:71
  361.4 8.0 %copy-start.3 = (bf16[32,32,1024]{2,1,0:T(8,128)(2,1)S(1)}, bf16[32,32,1024]{2,1,0:T(8,128)(2,1)}, u32[]{:S(2)}) copy-start(bf16[32,32,1024]{2,1,0:T(8,128)(2,1)} %all_to_all.14) | copy-start | bytes 6291460
  361.4 8.0 %copy-start.5 = (f32[1024,1024]{1,0:T(8,128)S(1)}, f32[1024,1024]{1,0:T(8,128)}, u32[]{:S(2)}) copy-start(f32[1024,1024]{1,0:T(8,128)} %param.15) | copy-start | bytes 12582916
  369.4 24.9 %copy-start.1 = (bf16[1024,1024]{1,0:T(8,128)(2,1)S(1)}, bf16[1024,1024]{1,0:T(8,128)(2,1)}, u32[]{:S(2)}) copy-start(bf16[1024,1024]{1,0:T(8,128)(2,1)} %param.17) | copy-start | bytes 6291460
Sparse Core Ops, SparseCore 0:
  26.3 78.2 all-gather.2
  156.8 154.2 reduce-scatter.1
